TPU v7x, 256 devices: a whole 4x4x8 slice. The times are simulated.
256 devices in a mesh: section: 8 (over z), expert: 8 (over x, core), dp: 4 (over y).
Axes of the slice: x: 4, y: 4, z: 8, core: 2. Of those that a mesh axis runs over, the one named last changes fastest.
Arguments:
- in_flight: bfloat16 [2, 8, 1024, 1536], P(None, 'section', ('expert', 'dp')), may hold values from -6 to 6
- entering: bfloat16 [1, 1024, 1536], P(None, ('expert', 'dp')), may hold values from -6 to 6
- checkpoints: bfloat16 [2, 2, 8, 1024, 1536], P(None, None, 'section', ('expert', 'dp')), may hold values from -6 to 6
- expert_ids: int32 [2, 2, 8, 1024, 2], P(None, None, 'section', ('expert', 'dp')), may hold values from 0 to 7, all different within a row; in each aligned block of 32 rows (0 to 31, 32 to 63, ..., all dimensions but the last counted through in order) at most 9 rows name the same one
- gates: float32 [2, 2, 8, 1024, 2], P(None, None, 'section', ('expert', 'dp')), may hold values from 0.1 to 1
- w_in: bfloat16 [2, 8, 8, 1536, 1536], P(None, 'section', 'expert', None, 'dp'), may hold values from -0.15625 to 0.15625
- w_out: bfloat16 [2, 8, 8, 1536, 1536], P(None, 'section', 'expert', 'dp'), may hold values from -0.15625 to 0.15625
Outputs:
- out_grads: bfloat16 [2, 2, 8, 1024, 1536], P(None, None, 'section', ('expert', 'dp'))
- w_in_grad: bfloat16 [2, 8, 8, 1536, 1536], P(None, 'section', 'expert', None, 'dp')
- w_out_grad: bfloat16 [2, 8, 8, 1536, 1536], P(None, 'section', 'expert', 'dp')
Inputs may be any that keep to these rules, and one draw needn't show every extreme that they name: `expert_ids`: in every tick, layer index and section, the 32 tokens of one device name each expert at most 9 times, a bound that some block reaches; the 2 experts of a token differ.
All inputs are finite; a program needn't handle non-finite values.
Results may differ from a plain program's by a relative error of at most 0.009.
Values may be sent and summed in bfloat16 or wider, within the bound.
A program may use at most 128 MiB of HBM per device.

v0:
```python
import jax
import jax.numpy as jnp
from jax import lax
from jax.experimental import pallas as pl
from jax.experimental.pallas import tpu as pltpu
from jax.sharding import PartitionSpec as P

MESH = pl.DeviceIdType.MESH
BF, F32, I32 = jnp.bfloat16, jnp.float32, jnp.int32


def iota(shape, dim):
    return lax.broadcasted_iota(I32, shape, dim)


def ones_at(cond):
    return jnp.where(cond, 1.0, 0.0).astype(BF)


def dot(a, b, dims=((1,), (0,))):
    return lax.dot_general(a, b, (dims, ((), ())), preferred_element_type=F32)


def kernel(
    flight, entering, chk, ids, gat, idc, w_in, w_out,
    out, gin, gout,
    W1, W2, XT, XS, XST, XB, XTR, IDX, GS, GR, GB, PG, AC, PR, RA, SB, FR, RS, RR, INC, RES, SELG, SELP, WG1, WG2,
    send_sem, loc_sem, id_sem, xa_sem, xf_sem, xm_sem, xt_sem, gx_sem, ga_sem, gf_sem, r1_sem, re_sem, r2_sem, rr_sem, z_sem,
    w_sem, o_sem,
):
    D = flight.shape[2]
    H = D // 2
    NJ = D // 128
    Q = D // 4
    z, e, y = (lax.axis_index(a) for a in ("section", "expert", "dp"))
    yn, yp, y2 = lax.rem(y + 1, 4), lax.rem(y + 3, 4), lax.rem(y + 2, 4)
    above, below, across = (z, e, yn), (z, e, yp), (z, e, y2)
    z_up, z_down = (lax.rem(z + 1, 8), e, y), (lax.rem(z + 7, 8), e, y)
    peers = [lax.rem(e + k, 8) for k in (1, 7, 2, 6, 3, 5, 4)]

    sends, locals_ = [], []

    def send(src, dst, sem, device):
        copy = pltpu.make_async_remote_copy(
            src_ref=src, dst_ref=dst, send_sem=send_sem.at[len(sends)], recv_sem=sem,
            device_id=device, device_id_type=MESH,
        )
        copy.start()
        sends.append(copy)

    def arrived(ref, sem):
        pltpu.make_async_copy(ref, ref, sem).wait()

    weights = []
    for c in (1, 0):
        weights.append((
            pltpu.make_async_copy(w_in.at[c], W1.at[c], w_sem.at[c, 0]),
            pltpu.make_async_copy(w_out.at[c], W2.at[c], w_sem.at[c, 1]),
        ))
        for copy in weights[-1]:
            copy.start()

    barrier = pltpu.get_barrier_semaphore()
    greeted = [(z, p, y) for p in peers] + [above, below, across, z_up, z_down]
    for device in greeted:
        pl.semaphore_signal(barrier, inc=1, device_id=device, device_id_type=MESH)

    for i in range(4):
        XT[i, y] = chk[i]
    IDX[y] = ids[:, 0:128]
    row, col = iota((384, 512), 0), iota((384, 512), 1)
    SELG[...] = ones_at(((row >> 5) == (col & 15)) & (((row >> 2) & 7) == ((col >> 4) & 7)) & ((row & 3) == (col >> 7)))
    row, col = iota((512, 384), 0), iota((512, 384), 1)
    SELP[...] = ones_at(((col >> 5) == (row & 15)) & (((col >> 2) & 7) == ((row >> 4) & 7)) & ((col & 3) == (row >> 7)))

    pl.semaphore_wait(barrier, len(greeted))

    def ids_send():
        for n, device in enumerate((above, below, across)):
            send(IDX.at[y], IDX.at[y], id_sem.at[n], device)

    def ids_wait():
        for n, b in enumerate((yp, yn, y2)):
            arrived(IDX.at[b], id_sem.at[n])

    def x_send(i):
        send(XT.at[i, y], XT.at[i, y], xa_sem.at[i, 0], above)
        send(XT.at[i, y], XT.at[i, y], xa_sem.at[i, 1], below)

    def x_forward(i):
        arrived(XT.at[i, yp], xa_sem.at[i, 0])
        half = XT.at[i, yp, pl.ds(0, 16)]
        send(half, half, xf_sem.at[i, 0], above)
        arrived(XT.at[i, yn], xa_sem.at[i, 1])
        half = XT.at[i, yn, pl.ds(16, 16)]
        send(half, half, xf_sem.at[i, 1], below)

    def x_dispatch(i):
        c, t = i // 2, i % 2
        r = 2 * (2 * t + c)
        arrived(XT.at[i, y2, pl.ds(0, 16)], xf_sem.at[i, 0])
        arrived(XT.at[i, y2, pl.ds(16, 16)], xf_sem.at[i, 1])
        lane = iota((8, 128), 1) >> 5
        every = jnp.where(lane == 0, IDX[0], jnp.where(lane == 1, IDX[1], jnp.where(lane == 2, IDX[2], IDX[3])))
        id0, id1 = every[r:r + 1], every[r + 1:r + 2]
        a, b = iota((128, 128), 0), iota((128, 128), 1)
        upper = ones_at(((a >> 5) == (b >> 5)) & (a < b))
        tokens = XT[i].reshape(128, D)
        row, col = iota((256, 128), 0), iota((256, 128), 1)
        member = ((id0 == (row >> 5)) | (id1 == (row >> 5))) & (((row >> 3) & 3) == (col >> 5))
        before = dot(ones_at(member), upper)
        hit = member & (before == (row & 7).astype(F32))
        XS[i] = dot(ones_at(hit), tokens).astype(BF).reshape(8, 32, D)
        row, col = iota((128, 128), 0), iota((128, 128), 1)
        member = ((id0 == (row >> 4)) | (id1 == (row >> 4))) & ((row & 3) == (col >> 5))
        before = dot(ones_at(member), upper)
        hit = member & (before == 8.0)
        wide = jnp.concatenate([ones_at(hit & (((row >> 2) & 3) == q)) for q in range(4)], axis=1)
        stacked = jnp.concatenate([tokens[:, Q * q:Q * q + Q] for q in range(4)], axis=0)
        XST[i] = dot(wide, stacked).astype(BF).reshape(8, 16, Q)
        for p in peers:
            send(XS.at[i, p], XB.at[i, e], xm_sem.at[i], (z, p, y))
            send(XST.at[i, p], XTR.at[i, e], xt_sem.at[i], (z, p, y))
        pltpu.make_async_copy(XS.at[i, e], XB.at[i, e], xm_sem.at[i]).start()
        pltpu.make_async_copy(XST.at[i, e], XTR.at[i, e], xt_sem.at[i]).start()

    def x_finish(i):
        arrived(XB.at[i, pl.ds(0, 8)], xm_sem.at[i])
        arrived(XTR.at[i], xt_sem.at[i])
        row, col = iota((128, 128), 0), iota((128, 128), 1)
        pick = ones_at(((row >> 5) == ((col >> 2) & 3)) & (((row >> 2) & 7) == (col >> 4)) & ((row & 3) == (col & 3)))
        rows = dot(pick, XTR[i].reshape(128, Q)).astype(BF)
        for q in range(4):
            XB[i, 8, :, Q * q:Q * q + Q] = rows[32 * q:32 * q + 32]

    def g_dispatch(i, incoming):
        c, t = i // 2, i % 2
        r = 2 * (2 * t + c)
        id0, id1 = ids[r:r + 1, 0:32], ids[r + 1:r + 2, 0:32]
        g0, g1 = gat[r:r + 1, :], gat[r + 1:r + 2, :]
        upper = ones_at(iota((32, 32), 0) < iota((32, 32), 1))
        row = iota((64, 32), 0)
        first = id0 == (row >> 3)
        member = first | (id1 == (row >> 3))
        before = dot(ones_at(member), upper)
        hit = member & (before == (row & 7).astype(F32))
        gate = jnp.sum(jnp.where(hit, jnp.where(first, g0, g1), 0.0), axis=1, keepdims=True)
        main = (dot(ones_at(hit), incoming) * gate).reshape(8, 8, D)
        GS[i, :, :, 0:H] = jnp.concatenate([main[:, :, :H], main[:, :, H:]], axis=1).astype(BF)
        row = iota((128, 32), 0)
        first = id0 == (row >> 4)
        member = first | (id1 == (row >> 4))
        counted = ones_at(member)
        before = dot(counted, upper)
        gate = jnp.sum(jnp.where(member & (before == 8.0), jnp.where(first, g0, g1), 0.0), axis=1, keepdims=True)
        row, col = iota((128, 32 * NJ), 0), iota((128, 32 * NJ), 1)
        wide0, wide1 = ids[r:r + 1, :], ids[r + 1:r + 2, :]
        member = (wide0 == (row >> 4)) | (wide1 == (row >> 4))
        upper = ones_at(iota((32, 32 * NJ), 0) < (iota((32, 32 * NJ), 1) & 31))
        before = dot(counted, upper)
        hit = member & (before == 8.0) & ((row & 15) == (col >> 5))
        stacked = jnp.concatenate([incoming[:, 128 * j:128 * j + 128] for j in range(NJ)], axis=0)
        GS[i, :, :, H:H + 128] = (dot(ones_at(hit), stacked) * gate).astype(BF).reshape(8, 16, 128)
        part = e >> 2
        for p in peers:
            send(GS.at[i, p], GR.at[i, y, e], gx_sem.at[i, part], (z, p, y))
        pltpu.make_async_copy(GS.at[i, e], GR.at[i, y, e], gx_sem.at[i, part]).start()

    def g_first(i):
        lower, upper = GR.at[i, y, pl.ds(0, 4)], GR.at[i, y, pl.ds(4, 4)]
        arrived(lower, gx_sem.at[i, 0])
        send(lower, lower, ga_sem.at[i, 0, 0], above)
        arrived(upper, gx_sem.at[i, 1])
        send(upper, upper, ga_sem.at[i, 1, 1], below)
        send(upper, upper, ga_sem.at[i, 0, 1], above)
        send(lower, lower, ga_sem.at[i, 1, 0], below)

    def g_second(i):
        lower, upper = GR.at[i, yp, pl.ds(0, 4)], GR.at[i, yn, pl.ds(4, 4)]
        arrived(lower, ga_sem.at[i, 0, 0])
        send(lower, lower, gf_sem.at[i, 0], above)
        arrived(upper, ga_sem.at[i, 1, 1])
        send(upper, upper, gf_sem.at[i, 1], below)

    def g_finish(i):
        arrived(GR.at[i, yp, pl.ds(4, 4)], ga_sem.at[i, 0, 1])
        arrived(GR.at[i, yn, pl.ds(0, 4)], ga_sem.at[i, 1, 0])
        arrived(GR.at[i, y2, pl.ds(0, 4)], gf_sem.at[i, 0])
        arrived(GR.at[i, y2, pl.ds(4, 4)], gf_sem.at[i, 1])

        @pl.loop(0, 8)
        def _(s):
            folded = GR[i, :, s, :, 0:H].astype(F32)
            GB[i, s, :, 0:H] = folded[:, 0:8].reshape(32, H).astype(BF)
            GB[i, s, :, H:D] = folded[:, 8:16].reshape(32, H).astype(BF)

        tails = dot(SELG[...], GR[i, :, :, :, H:H + 128].reshape(512, 128)).astype(BF)
        for j in range(NJ):
            GB[i, 8, :, 128 * j:128 * j + 128] = tails[32 * j:32 * j + 32]

    def compute(i):
        c = i // 2
        preact = dot(XB[i].reshape(288, D), W1[c])
        hidden = dot(GB[i].reshape(288, D), W2[c], ((1,), (1,)))
        squash = 1.0 / (1.0 + jnp.exp(-preact))
        AC[i] = (preact * squash).astype(BF)
        grad = (hidden * (squash * (1.0 + preact * (1.0 - squash)))).astype(BF)
        PG[i] = grad
        main = grad[0:256]
        left = dot(main, W1[c, 0:H], ((1,), (1,))).reshape(8, 4, 8, H)
        right = dot(main, W1[c, H:D], ((1,), (1,))).reshape(8, 4, 8, H)
        for b in range(4):
            PR[i, b, :, :, 0:H] = jnp.concatenate([left[:, b], right[:, b]], axis=1).astype(BF)
        tail = dot(grad[256:288], W1[c], ((1,), (1,))).astype(BF)
        stacked = jnp.concatenate([tail[:, 128 * j:128 * j + 128] for j in range(NJ)], axis=0)
        PR[i, :, :, :, H:H + 128] = dot(SELP[...], stacked).astype(BF).reshape(4, 8, 16, 128)

    def r_first(i):
        send(PR.at[i, y2, pl.ds(0, 4)], RA.at[i, 0], r1_sem.at[i, 0], above)
        send(PR.at[i, y2, pl.ds(4, 4)], RA.at[i, 1], r1_sem.at[i, 1], below)
        send(PR.at[i, yn, pl.ds(4, 4)], FR.at[i, 0, pl.ds(4, 4)], re_sem.at[i, 0], above)
        send(PR.at[i, yp, pl.ds(0, 4)], FR.at[i, 1, pl.ds(0, 4)], re_sem.at[i, 1], below)

    def r_second(i):
        arrived(RA.at[i, 0], r1_sem.at[i, 0])
        SB[i, 0] = (PR[i, yn, 0:4].astype(F32) + RA[i, 0].astype(F32)).astype(BF)
        send(SB.at[i, 0], FR.at[i, 0, pl.ds(0, 4)], r2_sem.at[i, 0], above)
        arrived(RA.at[i, 1], r1_sem.at[i, 1])
        SB[i, 1] = (PR[i, yp, 4:8].astype(F32) + RA[i, 1].astype(F32)).astype(BF)
        send(SB.at[i, 1], FR.at[i, 1, pl.ds(4, 4)], r2_sem.at[i, 1], below)

    def r_third(i):
        arrived(FR.at[i, 0, pl.ds(4, 4)], re_sem.at[i, 0])
        arrived(FR.at[i, 1, pl.ds(0, 4)], re_sem.at[i, 1])
        arrived(FR.at[i, 0, pl.ds(0, 4)], r2_sem.at[i, 0])
        arrived(FR.at[i, 1, pl.ds(4, 4)], r2_sem.at[i, 1])
        RS[i] = (PR[i, y].astype(F32) + FR[i, 0].astype(F32) + FR[i, 1].astype(F32)).astype(BF)
        for p in peers:
            send(RS.at[i, p], RR.at[i, e], rr_sem.at[i], (z, p, y))
        pltpu.make_async_copy(RS.at[i, e], RR.at[i, e], rr_sem.at[i]).start()

    def r_fourth(i, incoming):
        c, t = i // 2, i % 2
        id0, id1 = idc[2 * t + c, :, 0:1], idc[2 * t + c, :, 1:2]
        col = iota((32, 128), 1)
        member = (id0 == (col >> 4)) | (id1 == (col >> 4))
        before = dot(ones_at(iota((32, 32), 1) < iota((32, 32), 0)), ones_at(member))
        hit = member & (before == (col & 7).astype(F32))
        side = (col >> 3) & 1
        pick = jnp.concatenate([ones_at(hit & (side == 0)), ones_at(hit & (side == 1))], axis=0)
        last = member & (before == 8.0)
        pick_last = jnp.concatenate([ones_at(last & ((col & 15) == j)) for j in range(NJ)], axis=0)
        arrived(RR.at[i], rr_sem.at[i])
        main = dot(pick, RR[i, :, :, 0:H].reshape(128, H))
        tail = dot(pick_last, RR[i, :, :, H:H + 128].reshape(128, 128))
        for j in range(NJ):
            side = 128 * j // H
            at = 128 * j - side * H
            RES[i, :, 128 * j:128 * j + 128] = (
                incoming[:, 128 * j:128 * j + 128].astype(F32)
                + (main[32 * side:32 * side + 32, at:at + 128] + tail[32 * j:32 * j + 32])
            ).astype(BF)
        out[2 * t + c] = RES[i]

    outs = []

    def weight_grads(c):
        grad = PG[2 * c:2 * c + 2].reshape(576, -1)

        @pl.loop(0, D // 256)
        def _(n):
            at = pl.ds(pl.multiple_of(n * 256, 256), 256)
            WG1[c, at, :] = dot(XB[2 * c:2 * c + 2, :, :, at].reshape(576, 256), grad, ((0,), (0,))).astype(BF)

        copy = pltpu.make_async_copy(WG1.at[c], gin.at[c], o_sem.at[c, 0])
        copy.start()
        outs.append(copy)
        act = AC[2 * c:2 * c + 2].reshape(576, -1)

        @pl.loop(0, D // 512)
        def _(n):
            at = pl.ds(pl.multiple_of(n * 512, 512), 512)
            WG2[c, :, at] = dot(act, GB[2 * c:2 * c + 2, :, :, at].reshape(576, 512), ((0,), (0,))).astype(BF)

        copy = pltpu.make_async_copy(WG2.at[c], gout.at[c], o_sem.at[c, 1])
        copy.start()
        outs.append(copy)

    A, B, C, E = 2, 0, 3, 1
    ids_send()
    x_send(A)
    x_send(B)
    g_dispatch(A, flight[1])
    g_dispatch(B, flight[0])
    ids_wait()
    x_forward(A)
    x_forward(B)
    g_first(A)
    x_dispatch(A)
    g_second(A)
    g_first(B)
    x_dispatch(B)
    for copy in weights[0] + weights[1]:
        copy.wait()
    x_finish(A)
    g_finish(A)
    compute(A)
    r_first(A)
    g_second(B)
    x_send(C)
    x_finish(B)
    g_finish(B)
    r_second(A)
    compute(B)
    r_first(B)
    x_send(E)
    x_forward(C)
    r_third(A)
    r_second(B)
    r_fourth(A, flight[1])
    send(RES.at[A], INC.at[1], z_sem.at[1], z_up)
    x_dispatch(C)
    r_third(B)
    x_forward(E)
    arrived(INC.at[1], z_sem.at[1])
    upper = jnp.where(z == 0, entering[...], INC[1])
    g_dispatch(C, upper)
    r_fourth(B, flight[0])
    send(RES.at[B], INC.at[0], z_sem.at[0], z_down)
    g_first(C)
    arrived(INC.at[0], z_sem.at[0])
    lower = jnp.where(z == 7, RES[A], INC[0])
    g_dispatch(E, lower)
    x_dispatch(E)
    g_second(C)
    g_first(E)
    x_finish(C)
    g_finish(C)
    compute(C)
    r_first(C)
    g_second(E)
    x_finish(E)
    g_finish(E)
    r_second(C)
    compute(E)
    r_first(E)
    weight_grads(1)
    r_third(C)
    r_second(E)
    r_fourth(C, upper)
    weight_grads(0)
    r_third(E)
    r_fourth(E, lower)
    for copy in sends:
        copy.wait_send()
    for copy in outs:
        copy.wait()


def per_device(in_flight, entering, checkpoints, expert_ids, gates, w_in, w_out):
    D = in_flight.shape[-1]
    F = w_in.shape[-1]
    T = 4
    W = D // 2 + 128
    by_layer = checkpoints[:, :, 0].swapaxes(0, 1).reshape(T, 32, D)
    ids = expert_ids[:, :, 0]
    ids_rows = jnp.tile(ids.swapaxes(2, 3).reshape(2 * T, 32), (1, D // 128))
    gate_rows = gates[:, :, 0].swapaxes(2, 3).reshape(2 * T, 32)
    ids_columns = ids.reshape(T, 32, 2)
    vmem, anywhere = pl.BlockSpec(memory_space=pltpu.VMEM), pl.BlockSpec(memory_space=pl.ANY)
    dma = pltpu.SemaphoreType.DMA
    out, gin, gout = pl.pallas_call(
        kernel,
        out_shape=(
            jax.ShapeDtypeStruct((T, 32, D), BF),
            jax.ShapeDtypeStruct((2, D, F), BF),
            jax.ShapeDtypeStruct((2, F, D), BF),
        ),
        in_specs=[vmem] * 6 + [anywhere] * 2,
        out_specs=(vmem, anywhere, anywhere),
        scratch_shapes=[
            pltpu.VMEM((2, D, F), BF),
            pltpu.VMEM((2, F, D), BF),
            pltpu.VMEM((T, 4, 32, D), BF),
            pltpu.VMEM((T, 8, 32, D), BF),
            pltpu.VMEM((T, 8, 16, D // 4), BF),
            pltpu.VMEM((T, 9, 32, D), BF),
            pltpu.VMEM((T, 8, 16, D // 4), BF),
            pltpu.VMEM((4, 8, 128), I32),
            pltpu.VMEM((T, 8, 16, W), BF),
            pltpu.VMEM((T, 4, 8, 16, W), BF),
            pltpu.VMEM((T, 9, 32, D), BF),
            pltpu.VMEM((T, 288, F), BF),
            pltpu.VMEM((T, 288, F), BF),
            pltpu.VMEM((T, 4, 8, 16, W), BF),
            pltpu.VMEM((T, 2, 4, 16, W), BF),
            pltpu.VMEM((T, 2, 4, 16, W), BF),
            pltpu.VMEM((T, 2, 8, 16, W), BF),
            pltpu.VMEM((T, 8, 16, W), BF),
            pltpu.VMEM((T, 8, 16, W), BF),
            pltpu.VMEM((2, 32, D), BF),
            pltpu.VMEM((T, 32, D), BF),
            pltpu.VMEM((384, 512), BF),
            pltpu.VMEM((512, 384), BF),
            pltpu.VMEM((2, D, F), BF),
            pltpu.VMEM((2, F, D), BF),
            dma((200,)), dma((1,)), dma((3,)),
            dma((T, 2)), dma((T, 2)), dma((T,)), dma((T,)),
            dma((T, 2)), dma((T, 2, 2)), dma((T, 2)),
            dma((T, 2)), dma((T, 2)), dma((T, 2)), dma((T,)), dma((2,)),
            dma((2, 2)), dma((2, 2)),
        ],
        compiler_params=pltpu.CompilerParams(
            collective_id=0, has_side_effects=True, vmem_limit_bytes=60 * 2**20
        ),
    )(in_flight[:, 0], entering[0], by_layer, ids_rows, gate_rows, ids_columns, w_in[:, 0, 0], w_out[:, 0, 0])
    return out.reshape(2, 2, 1, 32, D), gin[:, None, None], gout[:, None, None]


def solution(mesh):
    tokens = P(None, None, "section", ("expert", "dp"), None)
    weight_in = P(None, "section", "expert", None, "dp")
    weight_out = P(None, "section", "expert", "dp", None)
    return jax.shard_map(
        per_device,
        mesh=mesh,
        in_specs=(P(None, "section", ("expert", "dp"), None), P(None, ("expert", "dp"), None), tokens, tokens, tokens,
                  weight_in, weight_out),
        out_specs=(tokens, weight_in, weight_out),
        check_vma=False,
    )
```

profile of v0, /device:TPU:1, one launch (start us, length us, event | category | flops | bytes accessed | tf_op | source)
XLA Modules:
  0.0 131.3 jit_solution(10690422747465664878)
XLA Ops:
  0.6 0.7 tile.11
  1.3 0.7 tile.12.ids
  2.0 1.4 %copy.16 = s32[2,2,1,32,2]{4,3,1,0,2:T(8,128)} copy(s32[2,2,1,32,2]{3,4,2,1,0:T(2,128)} %param.10) | data formatting | bytes 2048 | tf_op args[3]
  3.4 1.8 %copy.15 = bf16[2,2,32,1536]{3,2,1,0:T(8,128)(2,1)} copy(bf16[2,2,32,1536]{3,2,0,1:T(8,128)(2,1)} %bitcast.33) | data formatting | bytes 786432 | tf_op jit(solution)/shard_map/transpose | solution.py:365
  5.2 119.5 %shard_map.94 = (bf16[4,32,1536]{2,1,0:T(8,128)(2,1)}, bf16[2,1536,384]{2,1,0:T(8,128)(2,1)}, bf16[2,384,1536]{2,1,0:T(8,128)(2,1)}) custom-call(bf16[2,32,1536]{2,1,0:T(8,128)(2,1)} %bitcast.36, bf16[32,1536]{1,0:T(8,128)(2,1)} %bitcast.37, bf16[4,32,1536]{2,1,0:T(8,128)(2,1)} %bitcast.32, s32[8,384]{1,0:T(8,128)} %tile.12.ids, f32[8,32]{1,0:T(8,128)} %bitcast.39, ...), custom_call_target="tpu_custom_call" | custom-call | tf_op jit(solution)/shard_map/pallas_call | solution.py:372
  124.7 1.8 %copy.23 = bf16[2,2,1,32,1536]{4,3,2,1,0:T(8,128)(2,1)} copy(bf16[2,2,1,32,1536]{4,3,2,1,0:T(8,128)(2,1)} %bitcast.34) | data formatting | bytes 786432
  126.4 0.0 copy-start
  126.4 3.5 %copy.24 = bf16[2,1,1,1536,384]{4,3,2,1,0:T(8,128)(2,1)} copy(bf16[2,1,1,1536,384]{4,3,2,1,0:T(8,128)(2,1)} %bitcast.29) | data formatting | bytes 4718592
  129.9 0.0 copy-done
  129.9 1.4 %copy.25 = bf16[2,1,1,384,1536]{4,3,2,1,0:T(8,128)(2,1)} copy(bf16[2,1,1,384,1536]{4,3,2,1,0:T(8,128)(2,1)S(1)} %bitcast.28) | data formatting | bytes 4718592
Async XLA Ops:
  126.4 3.5 %copy-start = (bf16[2,384,1536]{2,1,0:T(8,128)(2,1)S(1)}, bf16[2,384,1536]{2,1,0:T(8,128)(2,1)}, u32[]{:S(2)}) copy-start(bf16[2,384,1536]{2,1,0:T(8,128)(2,1)} %get-tuple-element.8) | copy-start | bytes 7077892
where the time goes:
time: 132 us; the launch traced here: 131 us
  Pallas kernels  119 us (90%)
  local copies, waits for them, and re-layouts  11.2 us (8%)
    pallas_call x1, Pallas kernels, per_device(): pl.pallas_call(kernel, out_shape=(jax.ShapeDtypeStruct((T, 32, D), BF), j...  119 us
    unnamed x6, local copies, waits for them, and re-layouts  8.05 us

commit v1 on v0

v1 whole, which is shorter than its diff:
```python
import jax
import jax.numpy as jnp
from jax import lax
from jax.experimental import pallas as pl
from jax.experimental.pallas import tpu as pltpu
from jax.sharding import PartitionSpec as P

MESH = pl.DeviceIdType.MESH
BF, F32, I32 = jnp.bfloat16, jnp.float32, jnp.int32
NC = 2


def iota(shape, dim):
    return lax.broadcasted_iota(I32, shape, dim)


def ones_at(cond):
    return jnp.where(cond, 1.0, 0.0).astype(BF)


def dot(a, b, dims=((1,), (0,))):
    return lax.dot_general(a, b, (dims, ((), ())), preferred_element_type=F32)


def kernel(
    flight_in, entering_in, chk, ids_own, gat, w_in, w_out,
    out, gin, gout,
    flight, entering,
    W1, W2, XT, XS, XST, XB, XTR, IDX, GS, GR, GB, PG, AC, PR, RA, SB, FR, RS, RR, INC, RES, SELG, SELP, WG1, WG2, ids, idc, DG, GT, DL, GL, PK, PL, OUT,
    send_sem, loc_sem, id_sem, xa_sem, xf_sem, xm_sem, xt_sem, gx_sem, ga_sem, gf_sem, r1_sem, re_sem, r2_sem, rr_sem, z_sem,
    w_sem, o_sem, out_sem,
):
    D = flight.shape[2]
    H = D // 2
    K = H // NC
    to_expert = [pl.ds(K * k, K + 128 * (k == NC - 1)) for k in range(NC)]
    back = [pl.ds(128 * (k > 0) + K * k, K + 128 * (k == 0)) for k in range(NC)]
    NJ = D // 128
    Q = D // 4
    z, e, y = (lax.axis_index(a) for a in ("section", "expert", "dp"))
    yn, yp, y2 = lax.rem(y + 1, 4), lax.rem(y + 3, 4), lax.rem(y + 2, 4)
    above, below, across = (z, e, yn), (z, e, yp), (z, e, y2)
    z_up, z_down = (lax.rem(z + 1, 8), e, y), (lax.rem(z + 7, 8), e, y)
    peers = [lax.rem(e + k, 8) for k in (1, 7, 2, 6, 3, 5, 4)]

    sends, outs = [], []

    def send(src, dst, sem, device):
        copy = pltpu.make_async_remote_copy(
            src_ref=src, dst_ref=dst, send_sem=send_sem.at[len(sends)], recv_sem=sem,
            device_id=device, device_id_type=MESH,
        )
        copy.start()
        sends.append(copy)

    def arrived(ref, sem):
        pltpu.make_async_copy(ref, ref, sem).wait()

    barrier = pltpu.get_barrier_semaphore()
    greeted = [(z, p, y) for p in peers] + [above, below, across, z_up, z_down]
    for device in greeted:
        pl.semaphore_signal(barrier, inc=1, device_id=device, device_id_type=MESH)

    loads = [pltpu.make_async_copy(chk.at[2 * (i % 2) + i // 2], XT.at[i, y], loc_sem.at[i]) for i in range(4)]
    loads.append(pltpu.make_async_copy(flight_in, flight, loc_sem.at[4]))
    loads.append(pltpu.make_async_copy(entering_in, entering, loc_sem.at[5]))
    for copy in loads:
        copy.start()

    weights = []
    for c in (1, 0):
        weights.append((
            pltpu.make_async_copy(w_in.at[c], W1.at[c], w_sem.at[c, 0]),
            pltpu.make_async_copy(w_out.at[c], W2.at[c], w_sem.at[c, 1]),
        ))
        for copy in weights[-1]:
            copy.start()

    narrow = ids_own[...].astype(F32).astype(BF)
    ids[...] = dot(narrow, ones_at(iota((32, 32 * NJ), 0) == (iota((32, 32 * NJ), 1) & 31))).astype(I32)
    idc[...] = dot(ones_at(iota((32, 32), 0) == iota((32, 32), 1)), narrow, ((1,), (1,))).astype(I32)
    IDX[y] = ids[:, 0:128]
    row, col = iota((384, 512), 0), iota((384, 512), 1)
    SELG[...] = ones_at(((row >> 5) == (col & 15)) & (((row >> 2) & 7) == ((col >> 4) & 7)) & ((row & 3) == (col >> 7)))
    row, col = iota((512, 384), 0), iota((512, 384), 1)
    SELP[...] = ones_at(((col >> 5) == (row & 15)) & (((col >> 2) & 7) == ((row >> 4) & 7)) & ((col & 3) == (row >> 7)))

    def ids_send():
        for n, device in enumerate((above, below, across)):
            send(IDX.at[y], IDX.at[y], id_sem.at[n], device)

    def ids_wait():
        for n, b in enumerate((yp, yn, y2)):
            arrived(IDX.at[b], id_sem.at[n])

    def x_send(i):
        send(XT.at[i, y], XT.at[i, y], xa_sem.at[i, 0], above)
        send(XT.at[i, y], XT.at[i, y], xa_sem.at[i, 1], below)

    def x_forward(i):
        arrived(XT.at[i, yp], xa_sem.at[i, 0])
        half = XT.at[i, yp, pl.ds(0, 16)]
        send(half, half, xf_sem.at[i, 0], above)
        arrived(XT.at[i, yn], xa_sem.at[i, 1])
        half = XT.at[i, yn, pl.ds(16, 16)]
        send(half, half, xf_sem.at[i, 1], below)

    def x_dispatch(i, n):
        c, t = i // 2, i % 2
        r = 2 * (2 * t + c)
        a, b = iota((128, 128), 0), iota((128, 128), 1)
        upper = ones_at(((a >> 5) == (b >> 5)) & (a < b))
        pair = y // 2 if n == 0 else 1 - y // 2
        if n:
            arrived(XT.at[i, y2, pl.ds(0, 16)], xf_sem.at[i, 0])
            arrived(XT.at[i, y2, pl.ds(16, 16)], xf_sem.at[i, 1])
        both = jnp.where(iota((8, 128), 1) < 32, IDX[2 * pair], IDX[2 * pair + 1])
        id0, id1 = both[r:r + 1, 0:64], both[r + 1:r + 2, 0:64]
        row, col = iota((128, 64), 0), iota((128, 64), 1)
        member = ((id0 == (row >> 4)) | (id1 == (row >> 4))) & (((row >> 3) & 1) == (col >> 5))
        before = dot(ones_at(member), upper[0:64, 0:64])
        hit = member & (before == (row & 7).astype(F32))
        XS[i, pair] = dot(ones_at(hit), XT[i, pl.ds(2 * pair, 2)].reshape(64, D)).astype(BF).reshape(8, 16, D)
        rows = pl.ds(pl.multiple_of(16 * pair, 16), 16)
        for p in peers:
            send(XS.at[i, pair, p], XB.at[i, e, rows], xm_sem.at[i], (z, p, y))
        pltpu.make_async_copy(XS.at[i, pair, e], XB.at[i, e, rows], xm_sem.at[i]).start()
        if n:
            tokens = XT[i].reshape(128, D)
            lane = iota((8, 128), 1) >> 5
            every = jnp.where(lane == 0, IDX[0], jnp.where(lane == 1, IDX[1], jnp.where(lane == 2, IDX[2], IDX[3])))
            id0, id1 = every[r:r + 1], every[r + 1:r + 2]
            row, col = iota((128, 128), 0), iota((128, 128), 1)
            member = ((id0 == (row >> 4)) | (id1 == (row >> 4))) & ((row & 3) == (col >> 5))
            before = dot(ones_at(member), upper)
            hit = member & (before == 8.0)
            wide = jnp.concatenate([ones_at(hit & (((row >> 2) & 3) == q)) for q in range(4)], axis=1)
            stacked = jnp.concatenate([tokens[:, Q * q:Q * q + Q] for q in range(4)], axis=0)
            XST[i] = dot(wide, stacked).astype(BF).reshape(8, 16, Q)
            for p in peers:
                send(XST.at[i, p], XTR.at[i, e], xt_sem.at[i], (z, p, y))
            pltpu.make_async_copy(XST.at[i, e], XTR.at[i, e], xt_sem.at[i]).start()

    def x_finish(i):
        arrived(XB.at[i, pl.ds(0, 8)], xm_sem.at[i])
        arrived(XTR.at[i], xt_sem.at[i])
        row, col = iota((128, 128), 0), iota((128, 128), 1)
        pick = ones_at(((row >> 5) == ((col >> 2) & 3)) & (((row >> 2) & 7) == (col >> 4)) & ((row & 3) == (col & 3)))
        rows = dot(pick, XTR[i].reshape(128, Q)).astype(BF)
        for q in range(4):
            XB[i, 8, :, Q * q:Q * q + Q] = rows[32 * q:32 * q + 32]

    def prepare(i):
        c, t = i // 2, i % 2
        r = 2 * (2 * t + c)
        id0, id1 = ids[r:r + 1, 0:32], ids[r + 1:r + 2, 0:32]
        g0, g1 = gat[r:r + 1, :], gat[r + 1:r + 2, :]
        upper = ones_at(iota((32, 32), 0) < iota((32, 32), 1))
        row = iota((64, 32), 0)
        first = id0 == (row >> 3)
        member = first | (id1 == (row >> 3))
        before = dot(ones_at(member), upper)
        hit = member & (before == (row & 7).astype(F32))
        gate = jnp.sum(jnp.where(hit, jnp.where(first, g0, g1), 0.0), axis=1, keepdims=True)
        DG[i] = ones_at(hit)
        GT[i] = jnp.broadcast_to(gate, (64, 128))
        row = iota((128, 32), 0)
        first = id0 == (row >> 4)
        member = first | (id1 == (row >> 4))
        counted = ones_at(member)
        before = dot(counted, upper)
        gate = jnp.sum(jnp.where(member & (before == 8.0), jnp.where(first, g0, g1), 0.0), axis=1, keepdims=True)
        row, col = iota((128, 32 * NJ), 0), iota((128, 32 * NJ), 1)
        wide0, wide1 = ids[r:r + 1, :], ids[r + 1:r + 2, :]
        member = (wide0 == (row >> 4)) | (wide1 == (row >> 4))
        upper = ones_at(iota((32, 32 * NJ), 0) < (iota((32, 32 * NJ), 1) & 31))
        before = dot(counted, upper)
        DL[i] = ones_at(member & (before == 8.0) & ((row & 15) == (col >> 5)))
        GL[i] = jnp.broadcast_to(gate, (128, 128))

    def prepare_return(i):
        c, t = i // 2, i % 2
        r = 2 * (2 * t + c)
        id0, id1 = idc[:, r:r + 1], idc[:, r + 1:r + 2]
        col = iota((32, 128), 1)
        member = (id0 == (col >> 4)) | (id1 == (col >> 4))
        before = dot(ones_at(iota((32, 32), 1) < iota((32, 32), 0)), ones_at(member))
        hit = member & (before == (col & 7).astype(F32))
        side = (col >> 3) & 1
        PK[i] = jnp.concatenate([ones_at(hit & (side == 0)), ones_at(hit & (side == 1))], axis=0)
        last = member & (before == 8.0)
        PL[i] = jnp.concatenate([ones_at(last & ((col & 15) == j)) for j in range(NJ)], axis=0)

    def g_dispatch(i, k, piece):
        gate = jnp.concatenate([GT[i]] * (K // 128), axis=1)
        left = (dot(DG[i], piece(k, 0)) * gate).reshape(8, 8, K)
        right = (dot(DG[i], piece(k, 1)) * gate).reshape(8, 8, K)
        GS[i, :, :, K * k:K * k + K] = jnp.concatenate([left, right], axis=1).astype(BF)
        if k == NC - 1:
            stacked = jnp.concatenate(
                [piece(n, h)[:, 128 * m:128 * m + 128] for h in range(2) for n in range(NC) for m in range(K // 128)],
                axis=0,
            )
            GS[i, :, :, H:H + 128] = (dot(DL[i], stacked) * GL[i]).astype(BF).reshape(8, 16, 128)
        part, lanes = e // 4, to_expert[k]
        for p in peers:
            send(GS.at[i, p, :, lanes], GR.at[i, y, e, :, lanes], gx_sem.at[i, part, k], (z, p, y))
        pltpu.make_async_copy(GS.at[i, e, :, lanes], GR.at[i, y, e, :, lanes], gx_sem.at[i, part, k]).start()

    def g_first(i, k):
        lower, upper = GR.at[i, y, pl.ds(0, 4), :, to_expert[k]], GR.at[i, y, pl.ds(4, 4), :, to_expert[k]]
        arrived(lower, gx_sem.at[i, 0, k])
        send(lower, lower, ga_sem.at[i, 0, 0, k], above)
        arrived(upper, gx_sem.at[i, 1, k])
        send(upper, upper, ga_sem.at[i, 1, 1, k], below)
        send(upper, upper, ga_sem.at[i, 0, 1, k], above)
        send(lower, lower, ga_sem.at[i, 1, 0, k], below)

    def g_second(i, k):
        lower, upper = GR.at[i, yp, pl.ds(0, 4), :, to_expert[k]], GR.at[i, yn, pl.ds(4, 4), :, to_expert[k]]
        arrived(lower, ga_sem.at[i, 0, 0, k])
        send(lower, lower, gf_sem.at[i, 0, k], above)
        arrived(upper, ga_sem.at[i, 1, 1, k])
        send(upper, upper, gf_sem.at[i, 1, k], below)

    def g_finish(i, k):
        lanes = to_expert[k]
        arrived(GR.at[i, yp, pl.ds(4, 4), :, lanes], ga_sem.at[i, 0, 1, k])
        arrived(GR.at[i, yn, pl.ds(0, 4), :, lanes], ga_sem.at[i, 1, 0, k])
        arrived(GR.at[i, y2, pl.ds(0, 4), :, lanes], gf_sem.at[i, 0, k])
        arrived(GR.at[i, y2, pl.ds(4, 4), :, lanes], gf_sem.at[i, 1, k])

        @pl.loop(0, 8)
        def _(s):
            folded = GR[i, :, s, :, K * k:K * k + K].astype(F32)
            GB[i, s, :, K * k:K * k + K] = folded[:, 0:8].reshape(32, K).astype(BF)
            GB[i, s, :, H + K * k:H + K * k + K] = folded[:, 8:16].reshape(32, K).astype(BF)

        if k == NC - 1:
            tails = dot(SELG[...], GR[i, :, :, :, H:H + 128].reshape(512, 128)).astype(BF)
            for j in range(NJ):
                GB[i, 8, :, 128 * j:128 * j + 128] = tails[32 * j:32 * j + 32]

    def compute_a(i):
        c = i // 2
        preact = dot(XB[i].reshape(288, D), W1[c])
        hidden = dot(GB[i].reshape(288, D), W2[c], ((1,), (1,)))
        squash = 1.0 / (1.0 + jnp.exp(-preact))
        AC[i] = (preact * squash).astype(BF)
        grad = (hidden * (squash * (1.0 + preact * (1.0 - squash)))).astype(BF)
        PG[i] = grad

    def compute_b(i, k):
        c = i // 2
        main = PG[i, 0:256]
        left = dot(main, W1[c, K * k:K * k + K], ((1,), (1,))).reshape(8, 4, 8, K)
        right = dot(main, W1[c, H + K * k:H + K * k + K], ((1,), (1,))).reshape(8, 4, 8, K)
        for b in range(4):
            PR[i, b, :, :, 128 + K * k:128 + K * k + K] = jnp.concatenate([left[:, b], right[:, b]], axis=1).astype(BF)
        if k == 0:
            tail = dot(PG[i, 256:288], W1[c], ((1,), (1,))).astype(BF)
            stacked = jnp.concatenate([tail[:, 128 * j:128 * j + 128] for j in range(NJ)], axis=0)
            PR[i, :, :, :, 0:128] = dot(SELP[...], stacked).astype(BF).reshape(4, 8, 16, 128)
        r_first(i, k)

    def r_first(i, k):
        lanes, lower, upper = back[k], pl.ds(0, 4), pl.ds(4, 4)
        send(PR.at[i, y2, lower, :, lanes], RA.at[i, 0, :, :, lanes], r1_sem.at[i, 0, k], above)
        send(PR.at[i, y2, upper, :, lanes], RA.at[i, 1, :, :, lanes], r1_sem.at[i, 1, k], below)
        send(PR.at[i, yn, upper, :, lanes], FR.at[i, 0, upper, :, lanes], re_sem.at[i, 0, k], above)
        send(PR.at[i, yp, lower, :, lanes], FR.at[i, 1, lower, :, lanes], re_sem.at[i, 1, k], below)

    def r_second(i, k):
        lanes, lower, upper = back[k], pl.ds(0, 4), pl.ds(4, 4)
        arrived(RA.at[i, 0, :, :, lanes], r1_sem.at[i, 0, k])
        SB[i, 0, :, :, lanes] = (PR[i, yn, 0:4, :, lanes].astype(F32) + RA[i, 0, :, :, lanes].astype(F32)).astype(BF)
        send(SB.at[i, 0, :, :, lanes], FR.at[i, 0, lower, :, lanes], r2_sem.at[i, 0, k], above)
        arrived(RA.at[i, 1, :, :, lanes], r1_sem.at[i, 1, k])
        SB[i, 1, :, :, lanes] = (PR[i, yp, 4:8, :, lanes].astype(F32) + RA[i, 1, :, :, lanes].astype(F32)).astype(BF)
        send(SB.at[i, 1, :, :, lanes], FR.at[i, 1, upper, :, lanes], r2_sem.at[i, 1, k], below)

    def r_third(i, k):
        lanes, lower, upper = back[k], pl.ds(0, 4), pl.ds(4, 4)
        arrived(FR.at[i, 0, upper, :, lanes], re_sem.at[i, 0, k])
        arrived(FR.at[i, 1, lower, :, lanes], re_sem.at[i, 1, k])
        arrived(FR.at[i, 0, lower, :, lanes], r2_sem.at[i, 0, k])
        arrived(FR.at[i, 1, upper, :, lanes], r2_sem.at[i, 1, k])
        RS[i, :, :, lanes] = (
            PR[i, y, :, :, lanes].astype(F32) + FR[i, 0, :, :, lanes].astype(F32) + FR[i, 1, :, :, lanes].astype(F32)
        ).astype(BF)
        for p in peers:
            send(RS.at[i, p, :, lanes], RR.at[i, e, :, lanes], rr_sem.at[i, k], (z, p, y))
        pltpu.make_async_copy(RS.at[i, e, :, lanes], RR.at[i, e, :, lanes], rr_sem.at[i, k]).start()

    def r_fourth(i, k, piece):
        c, t = i // 2, i % 2
        arrived(RR.at[i, :, :, back[k]], rr_sem.at[i, k])
        main = dot(PK[i], RR[i, :, :, 128 + K * k:128 + K * k + K].reshape(128, K))
        per = K // 128
        for h in range(2):
            j = NJ // 2 * h + per * k
            tail = dot(PL[i, 32 * j:32 * j + 32 * per], RR[i, :, :, 0:128].reshape(128, 128))
            own = piece(k, h).astype(F32)
            for m in range(per):
                at = slice(128 * m, 128 * m + 128)
                RES[i, k, h, :, at] = (own[:, at] + (main[32 * h:32 * h + 32, at] + tail[32 * m:32 * m + 32])).astype(BF)
            OUT[i, :, H * h + K * k:H * h + K * k + K] = RES[i, k, h]
        if k == NC - 1:
            copy = pltpu.make_async_copy(OUT.at[i], out.at[2 * t + c], out_sem.at[i])
            copy.start()
            outs.append(copy)

    def grads_in(c, n, count):
        grad = PG[2 * c:2 * c + 2].reshape(576, -1)

        @pl.loop(n, n + count)
        def _(n):
            at = pl.ds(pl.multiple_of(n * 256, 256), 256)
            WG1[c, at, :] = dot(XB[2 * c:2 * c + 2, :, :, at].reshape(576, 256), grad, ((0,), (0,))).astype(BF)

        if n + count == D // 256:
            copy = pltpu.make_async_copy(WG1.at[c], gin.at[c], o_sem.at[c, 0])
            copy.start()
            outs.append(copy)

    def grads_out(c, n):
        at = pl.ds(512 * n, 512)
        act = AC[2 * c:2 * c + 2].reshape(576, -1)
        WG2[c, :, at] = dot(act, GB[2 * c:2 * c + 2, :, :, at].reshape(576, 512), ((0,), (0,))).astype(BF)
        if n == D // 512 - 1:
            copy = pltpu.make_async_copy(WG2.at[c], gout.at[c], o_sem.at[c, 1])
            copy.start()
            outs.append(copy)

    def from_flight(c):
        return lambda k, h: flight[c, :, H * h + K * k:H * h + K * k + K]

    def upper_piece(k, h):
        return jnp.where(z == 0, entering[:, H * h + K * k:H * h + K * k + K], INC[1, k, h])

    def lower_piece(k, h):
        return jnp.where(z == 7, RES[2, k, h], INC[0, k, h])

    def pass_up(k):
        send(RES.at[A, k], INC.at[1, k], z_sem.at[1, k], z_up)

    def pass_down(k):
        send(RES.at[B, k], INC.at[0, k], z_sem.at[0, k], z_down)

    def from_below(k):
        arrived(INC.at[1, k], z_sem.at[1, k])

    def from_above(k):
        arrived(INC.at[0, k], z_sem.at[0, k])

    A, B, C, E = 2, 0, 3, 1
    flight1, flight0 = from_flight(1), from_flight(0)
    each = range(NC)
    prepare(A)
    prepare(B)
    for copy in loads:
        copy.wait()
    pl.semaphore_wait(barrier, len(greeted))
    ids_send()
    x_send(A)
    x_send(B)
    for k in each:
        g_dispatch(A, k, flight1)
    for k in each:
        g_dispatch(B, k, flight0)
    ids_wait()
    x_forward(A)
    x_dispatch(A, 0)
    for k in each:
        g_first(A, k)
    x_forward(B)
    x_dispatch(A, 1)
    g_second(A, 0)
    x_send(C)
    for k in each[1:]:
        g_second(A, k)
    for k in each:
        g_first(B, k)
    x_dispatch(B, 0)
    x_dispatch(B, 1)
    prepare_return(A)
    prepare(C)
    x_forward(C)
    for copy in weights[0] + weights[1]:
        copy.wait()
    x_finish(A)
    for k in each:
        g_finish(A, k)
    compute_a(A)
    for k in each:
        compute_b(A, k)
    for k in each:
        g_second(B, k)
    r_second(A, 0)
    x_dispatch(C, 0)
    for k in each[1:]:
        r_second(A, k)
    x_send(E)
    for k in each:
        g_finish(B, k)
    x_finish(B)
    r_third(A, 0)
    compute_a(B)
    for k in each[1:]:
        r_third(A, k)
    for k in each:
        compute_b(B, k)
    for k in each:
        r_fourth(A, k, flight1)
        pass_up(k)
    x_dispatch(C, 1)
    x_forward(E)
    prepare_return(B)
    prepare(E)
    for k in each:
        r_second(B, k)
        from_below(k)
        g_dispatch(C, k, upper_piece)
    for k in each:
        r_third(B, k)
        g_first(C, k)
    x_dispatch(E, 0)
    for k in each:
        r_fourth(B, k, flight0)
        pass_down(k)
    prepare_return(C)
    prepare_return(E)
    for k in each:
        g_second(C, k)
        from_above(k)
        g_dispatch(E, k, lower_piece)
    x_dispatch(E, 1)
    x_finish(C)
    for k in each:
        g_finish(C, k)
    compute_a(C)
    for k in each:
        g_first(E, k)
        compute_b(C, k)
    grads_in(1, 0, 2)
    g_second(E, 0)
    grads_in(1, 2, 2)
    for k in each[1:]:
        g_second(E, k)
    grads_in(1, 4, 2)
    for k in each:
        r_second(C, k)
    grads_out(1, 0)
    x_finish(E)
    for k in each:
        g_finish(E, k)
    compute_a(E)
    for k in each:
        compute_b(E, k)
    for k in each:
        r_third(C, k)
    grads_out(1, 1)
    grads_out(1, 2)
    r_second(E, 0)
    grads_in(0, 0, 2)
    for k in each[1:]:
        r_second(E, k)
    for k in each:
        r_fourth(C, k, upper_piece)
    grads_in(0, 2, 4)
    for k in each:
        r_third(E, k)
        grads_out(0, k)
    grads_out(0, 2)
    for k in each:
        r_fourth(E, k, lower_piece)
    for copy in sends:
        copy.wait_send()
    for copy in outs:
        copy.wait()


def copier(a, b, c, a_out, b_out, c_out, a_held, b_held, c_held, in_sem, out_sem):
    parts = []
    for source, held, target in ((b, b_held, b_out), (c, c_held, c_out)):
        rows = source.shape[1] // 2
        for i in range(2):
            for n in range(2):
                at = (i, pl.ds(rows * n, rows))
                parts.append((source.at[at], held.at[at], target.at[at]))
    parts.append((a, a_held, a_out))
    loads = [pltpu.make_async_copy(x, v, in_sem.at[n]) for n, (x, v, _) in enumerate(parts)]
    stores = [pltpu.make_async_copy(v, w, out_sem.at[n]) for n, (_, v, w) in enumerate(parts)]
    for load in loads:
        load.start()
    for load, store in zip(loads, stores):
        load.wait()
        store.start()
    for store in stores:
        store.wait()


def per_device(in_flight, entering, checkpoints, expert_ids, gates, w_in, w_out):
    D = in_flight.shape[-1]
    F = w_in.shape[-1]
    T = 4
    W = D // 2 + 128
    K = D // 2 // NC
    ids = expert_ids[:, :, 0]
    ids_rows = ids.swapaxes(2, 3).reshape(2 * T, 32)
    gate_rows = gates[:, :, 0].swapaxes(2, 3).reshape(2 * T, 32)
    vmem, anywhere = pl.BlockSpec(memory_space=pltpu.VMEM), pl.BlockSpec(memory_space=pl.ANY)
    dma = pltpu.SemaphoreType.DMA
    out, gin, gout = pl.pallas_call(
        kernel,
        out_shape=(
            jax.ShapeDtypeStruct((T, 32, D), BF),
            jax.ShapeDtypeStruct((2, D, F), BF),
            jax.ShapeDtypeStruct((2, F, D), BF),
        ),
        in_specs=[anywhere] * 3 + [vmem] * 2 + [anywhere] * 2,
        out_specs=(anywhere, anywhere, anywhere),
        scratch_shapes=[
            pltpu.VMEM((2, 32, D), BF),
            pltpu.VMEM((32, D), BF),
            pltpu.VMEM((2, D, F), BF),
            pltpu.VMEM((2, F, D), BF),
            pltpu.VMEM((T, 4, 32, D), BF),
            pltpu.VMEM((T, 2, 8, 16, D), BF),
            pltpu.VMEM((T, 8, 16, D // 4), BF),
            pltpu.VMEM((T, 9, 32, D), BF),
            pltpu.VMEM((T, 8, 16, D // 4), BF),
            pltpu.VMEM((4, 8, 128), I32),
            pltpu.VMEM((T, 8, 16, W), BF),
            pltpu.VMEM((T, 4, 8, 16, W), BF),
            pltpu.VMEM((T, 9, 32, D), BF),
            pltpu.VMEM((T, 288, F), BF),
            pltpu.VMEM((T, 288, F), BF),
            pltpu.VMEM((T, 4, 8, 16, W), BF),
            pltpu.VMEM((T, 2, 4, 16, W), BF),
            pltpu.VMEM((T, 2, 4, 16, W), BF),
            pltpu.VMEM((T, 2, 8, 16, W), BF),
            pltpu.VMEM((T, 8, 16, W), BF),
            pltpu.VMEM((T, 8, 16, W), BF),
            pltpu.VMEM((2, NC, 2, 32, K), BF),
            pltpu.VMEM((T, NC, 2, 32, K), BF),
            pltpu.VMEM((384, 512), BF),
            pltpu.VMEM((512, 384), BF),
            pltpu.VMEM((2, D, F), BF),
            pltpu.VMEM((2, F, D), BF),
            pltpu.VMEM((8, D // 4), I32),
            pltpu.VMEM((32, 8), I32),
            pltpu.VMEM((T, 64, 32), BF),
            pltpu.VMEM((T, 64, 128), F32),
            pltpu.VMEM((T, 128, D // 4), BF),
            pltpu.VMEM((T, 128, 128), F32),
            pltpu.VMEM((T, 64, 128), BF),
            pltpu.VMEM((T, D // 4, 128), BF),
            pltpu.VMEM((T, 32, D), BF),
            dma((112 + 108 * NC,)), dma((6,)), dma((3,)),
            dma((T, 2)), dma((T, 2)), dma((T,)), dma((T,)),
            dma((T, 2, NC)), dma((T, 2, 2, NC)), dma((T, 2, NC)),
            dma((T, 2, NC)), dma((T, 2, NC)), dma((T, 2, NC)), dma((T, NC)), dma((2, NC)),
            dma((2, 2)), dma((2, 2)), dma((4,)),
        ],
        compiler_params=pltpu.CompilerParams(
            collective_id=0, has_side_effects=True, vmem_limit_bytes=60 * 2**20
        ),
    )(in_flight[:, 0], entering[0], checkpoints.reshape(T, 32, D), ids_rows, gate_rows, w_in[:, 0, 0], w_out[:, 0, 0])
    out, gin, gout = pl.pallas_call(
        copier,
        out_shape=tuple(jax.ShapeDtypeStruct(v.shape, v.dtype) for v in (out, gin, gout)),
        in_specs=[anywhere] * 3,
        out_specs=(anywhere,) * 3,
        scratch_shapes=[pltpu.VMEM(v.shape, v.dtype) for v in (out, gin, gout)] + [dma((9,)), dma((9,))],
        compiler_params=pltpu.CompilerParams(vmem_limit_bytes=60 * 2**20),
    )(out, gin, gout)
    return out.reshape(2, 2, 1, 32, D), gin[:, None, None], gout[:, None, None]


def solution(mesh):
    tokens = P(None, None, "section", ("expert", "dp"), None)
    weight_in = P(None, "section", "expert", None, "dp")
    weight_out = P(None, "section", "expert", "dp", None)
    return jax.shard_map(
        per_device,
        mesh=mesh,
        in_specs=(P(None, "section", ("expert", "dp"), None), P(None, ("expert", "dp"), None), tokens, tokens, tokens,
                  weight_in, weight_out),
        out_specs=(tokens, weight_in, weight_out),
        check_vma=False,
    )
```

time: 132 us -> 111 us (0.84)
  local copies, waits for them, and re-layouts: 11.2 us -> 0 us
  Pallas kernels: 119 us -> 110 us
    pallas_call x1, Pallas kernels: 119 us -> 106 us  [per_device(): pl.pallas_call(kernel, out_shape=(jax.ShapeDtypeStruct((T, 32, D), BF), j...]
    unnamed x6 -> x0, local copies, waits for them, and re-layouts: 8.05 us -> none
    pallas_call x0 -> x1, Pallas kernels: none -> 4.46 us  [per_device(): pl.pallas_call(copier, out_shape=tuple((jax.ShapeDtypeStruct(v.shape, v.d...]
    transpose x1 -> x0, local copies, waits for them, and re-layouts: 1.77 us -> none  [per_device(): by_layer = checkpoints[:, :, 0].swapaxes(0, 1).reshape(T, 32, D)]
    another operation x2 -> x0, local copies, waits for them, and re-layouts: 1.38 us -> none  [per_device(): ids_rows = jnp.tile(ids.swapaxes(2, 3).reshape(2 * T, 32), (1, D // 128))]
where the time goes in v1:
time: 111 us
  Pallas kernels  110 us (99%)
    pallas_call x1, Pallas kernels, per_device(): pl.pallas_call(kernel, out_shape=(jax.ShapeDtypeStruct((T, 32, D), BF), j...  106 us
    pallas_call x1, Pallas kernels, per_device(): pl.pallas_call(copier, out_shape=tuple((jax.ShapeDtypeStruct(v.shape, v.d...  4.46 us

profile of v1, /device:TPU:1, one launch (start us, length us, event | category | flops | bytes accessed | tf_op | source)
XLA Modules:
  0.0 111.0 jit_solution(10342473862251934018)
XLA Ops:
  0.6 105.7 %shard_map.94 = (bf16[4,32,1536]{2,1,0:T(8,128)(2,1)}, bf16[2,1536,384]{2,1,0:T(8,128)(2,1)}, bf16[2,384,1536]{2,1,0:T(8,128)(2,1)}) custom-call(bf16[2,32,1536]{2,1,0:T(8,128)(2,1)} %bitcast.27, bf16[32,1536]{1,0:T(8,128)(2,1)} %bitcast.28, bf16[4,32,1536]{2,1,0:T(8,128)(2,1)} %bitcast.26, s32[8,32]{1,0:T(8,128)} %bitcast.29, f32[8,32]{1,0:T(8,128)} %bitcast.30, ...), custom_call_target="tpu_custom_call" | custom-call | tf_op jit(solution)/shard_map/pallas_call | solution.py:514
  106.4 4.5 %shard_map.95 = (bf16[4,32,1536]{2,1,0:T(8,128)(2,1)}, bf16[2,1536,384]{2,1,0:T(8,128)(2,1)}, bf16[2,384,1536]{2,1,0:T(8,128)(2,1)}) custom-call(bf16[4,32,1536]{2,1,0:T(8,128)(2,1)} %get-tuple-element.9.a, bf16[2,1536,384]{2,1,0:T(8,128)(2,1)} %get-tuple-element.10.b, bf16[2,384,1536]{2,1,0:T(8,128)(2,1)} %get-tuple-element.11.c), custom_call_target="tpu_custom_call" | custom-call | tf_op jit(solution)/shard_map/pallas_call | solution.py:570

commit v2 on v1

--- a/solution.py
+++ b/solution.py
@@ -26,7 +26,7 @@
     flight_in, entering_in, chk, ids_own, gat, w_in, w_out,
     out, gin, gout,
     flight, entering,
-    W1, W2, XT, XS, XST, XB, XTR, IDX, GS, GR, GB, PG, AC, PR, RA, SB, FR, RS, RR, INC, RES, SELG, SELP, WG1, WG2, ids, idc, DG, GT, DL, GL, PK, PL, OUT,
+    W1, W2, XT, XS, XST, XB, XTR, IDX, GS, GR, GB, PG, AC, PR, RA, SB, FR, RS, RR, INC, RES, SELG, SELP, WG1, WG2, ids, idc, DG, GT, DL, GL, PK, PL, OUT, HELD,
     send_sem, loc_sem, id_sem, xa_sem, xf_sem, xm_sem, xt_sem, gx_sem, ga_sem, gf_sem, r1_sem, re_sem, r2_sem, rr_sem, z_sem,
     w_sem, o_sem, out_sem,
 ):
@@ -241,14 +241,26 @@
             for j in range(NJ):
                 GB[i, 8, :, 128 * j:128 * j + 128] = tails[32 * j:32 * j + 32]
 
-    def compute_a(i):
-        c = i // 2
-        preact = dot(XB[i].reshape(288, D), W1[c])
-        hidden = dot(GB[i].reshape(288, D), W2[c], ((1,), (1,)))
+    def hidden_of(i):
+        return dot(GB[i].reshape(288, D), W2[i // 2], ((1,), (1,)))
+
+    def slope_of(i):
+        preact = dot(XB[i].reshape(288, D), W1[i // 2])
         squash = 1.0 / (1.0 + jnp.exp(-preact))
         AC[i] = (preact * squash).astype(BF)
-        grad = (hidden * (squash * (1.0 + preact * (1.0 - squash)))).astype(BF)
-        PG[i] = grad
+        return squash * (1.0 + preact * (1.0 - squash))
+
+    def hidden_first(i):
+        HELD[i] = hidden_of(i)
+
+    def slope_last(i):
+        PG[i] = (HELD[i] * slope_of(i)).astype(BF)
+
+    def slope_first(i):
+        HELD[i] = slope_of(i)
+
+    def hidden_last(i):
+        PG[i] = (hidden_of(i) * HELD[i]).astype(BF)
 
     def compute_b(i, k):
         c = i // 2
@@ -388,10 +400,11 @@
     x_forward(C)
     for copy in weights[0] + weights[1]:
         copy.wait()
+    for k in each:
+        g_finish(A, k)
+    hidden_first(A)
     x_finish(A)
-    for k in each:
-        g_finish(A, k)
-    compute_a(A)
+    slope_last(A)
     for k in each:
         compute_b(A, k)
     for k in each:
@@ -400,16 +413,17 @@
     x_dispatch(C, 0)
     for k in each[1:]:
         r_second(A, k)
-    x_send(E)
     for k in each:
         g_finish(B, k)
+    hidden_first(B)
     x_finish(B)
     r_third(A, 0)
-    compute_a(B)
+    slope_last(B)
     for k in each[1:]:
         r_third(A, k)
     for k in each:
         compute_b(B, k)
+    x_send(E)
     for k in each:
         r_fourth(A, k, flight1)
         pass_up(k)
@@ -436,9 +450,10 @@
         g_dispatch(E, k, lower_piece)
     x_dispatch(E, 1)
     x_finish(C)
+    slope_first(C)
     for k in each:
         g_finish(C, k)
-    compute_a(C)
+    hidden_last(C)
     for k in each:
         g_first(E, k)
         compute_b(C, k)
@@ -452,9 +467,10 @@
         r_second(C, k)
     grads_out(1, 0)
     x_finish(E)
+    slope_first(E)
     for k in each:
         g_finish(E, k)
-    compute_a(E)
+    hidden_last(E)
     for k in each:
         compute_b(E, k)
     for k in each:
@@ -470,8 +486,8 @@
     grads_in(0, 2, 4)
     for k in each:
         r_third(E, k)
-        grads_out(0, k)
-    grads_out(0, 2)
+    for n in range(3):
+        grads_out(0, n)
     for k in each:
         r_fourth(E, k, lower_piece)
     for copy in sends:
@@ -483,9 +499,9 @@
 def copier(a, b, c, a_out, b_out, c_out, a_held, b_held, c_held, in_sem, out_sem):
     parts = []
     for source, held, target in ((b, b_held, b_out), (c, c_held, c_out)):
-        rows = source.shape[1] // 2
+        rows = source.shape[1]
         for i in range(2):
-            for n in range(2):
+            for n in range(1):
                 at = (i, pl.ds(rows * n, rows))
                 parts.append((source.at[at], held.at[at], target.at[at]))
     parts.append((a, a_held, a_out))
@@ -557,6 +573,7 @@
             pltpu.VMEM((T, 64, 128), BF),
             pltpu.VMEM((T, D // 4, 128), BF),
             pltpu.VMEM((T, 32, D), BF),
+            pltpu.VMEM((T, 288, F), F32),
             dma((112 + 108 * NC,)), dma((6,)), dma((3,)),
             dma((T, 2)), dma((T, 2)), dma((T,)), dma((T,)),
             dma((T, 2, NC)), dma((T, 2, 2, NC)), dma((T, 2, NC)),
@@ -572,7 +589,7 @@
         out_shape=tuple(jax.ShapeDtypeStruct(v.shape, v.dtype) for v in (out, gin, gout)),
         in_specs=[anywhere] * 3,
         out_specs=(anywhere,) * 3,
-        scratch_shapes=[pltpu.VMEM(v.shape, v.dtype) for v in (out, gin, gout)] + [dma((9,)), dma((9,))],
+        scratch_shapes=[pltpu.VMEM(v.shape, v.dtype) for v in (out, gin, gout)] + [dma((5,)), dma((5,))],
         compiler_params=pltpu.CompilerParams(vmem_limit_bytes=60 * 2**20),
     )(out, gin, gout)
     return out.reshape(2, 2, 1, 32, D), gin[:, None, None], gout[:, None, None]

time: 111 us -> 109 us (0.982)
  Pallas kernels: 110 us -> 108 us
    pallas_call x1, Pallas kernels: 106 us -> 104 us  [per_device(): pl.pallas_call(kernel, out_shape=(jax.ShapeDtypeStruct((T, 32, D), BF), j...]
where the time goes in v2:
time: 109 us
  Pallas kernels  108 us (99%)
    pallas_call x1, Pallas kernels, per_device(): pl.pallas_call(kernel, out_shape=(jax.ShapeDtypeStruct((T, 32, D), BF), j...  104 us
    pallas_call x1, Pallas kernels, per_device(): pl.pallas_call(copier, out_shape=tuple((jax.ShapeDtypeStruct(v.shape, v.d...  3.89 us

profile of v2, /device:TPU:1, one launch (start us, length us, event | category | flops | bytes accessed | tf_op | source)
XLA Modules:
  0.0 108.7 jit_solution(1075798473734103053)
XLA Ops:
  0.6 104.0 %shard_map.94 = (bf16[4,32,1536]{2,1,0:T(8,128)(2,1)}, bf16[2,1536,384]{2,1,0:T(8,128)(2,1)}, bf16[2,384,1536]{2,1,0:T(8,128)(2,1)}) custom-call(bf16[2,32,1536]{2,1,0:T(8,128)(2,1)} %bitcast.27, bf16[32,1536]{1,0:T(8,128)(2,1)} %bitcast.28, bf16[4,32,1536]{2,1,0:T(8,128)(2,1)} %bitcast.26, s32[8,32]{1,0:T(8,128)} %bitcast.29, f32[8,32]{1,0:T(8,128)} %bitcast.30, ...), custom_call_target="tpu_custom_call" | custom-call | tf_op jit(solution)/shard_map/pallas_call | solution.py:530
  104.6 3.9 %shard_map.95 = (bf16[4,32,1536]{2,1,0:T(8,128)(2,1)}, bf16[2,1536,384]{2,1,0:T(8,128)(2,1)}, bf16[2,384,1536]{2,1,0:T(8,128)(2,1)}) custom-call(bf16[4,32,1536]{2,1,0:T(8,128)(2,1)} %get-tuple-element.9.a, bf16[2,1536,384]{2,1,0:T(8,128)(2,1)} %get-tuple-element.10.b, bf16[2,384,1536]{2,1,0:T(8,128)(2,1)} %get-tuple-element.11.c), custom_call_target="tpu_custom_call" | custom-call | tf_op jit(solution)/shard_map/pallas_call | solution.py:587
